TPU v7x, 128 devices: a whole 4x4x4 slice. The times are simulated.
128 devices in a mesh: gx: 8 (over x_lo, y), gy: 4 (over x_hi, core), sa: 4 (over z).
Axes of the slice: x: 4 (x_hi: 2, x_lo: 2; x = x_hi * 2 + x_lo), y: 4, z: 4, core: 2. Of those that a mesh axis runs over, the one named last changes fastest.
Arguments:
- field: float32 [48, 2, 2048, 1024], P('sa', None, 'gx', 'gy'), may hold values from -6.8 to 6.8
- basis_species: float32 [48, 24], replicated, may hold values from -5 to 5
- basis_x: float32 [2048, 256], P('gx'), may hold values from -5 to 5
- basis_y: float32 [1024, 256], P(('gy', 'sa')), may hold values from -5 to 5
Outputs:
- core: float32 [256, 256, 24, 2], P(('gy', 'sa'), 'gx')
- factor_species: float32 [48, 24], replicated
- factor_x: float32 [2048, 256], P('gx')
- factor_y: float32 [1024, 256], P(('gy', 'sa'))
All inputs are finite; a program needn't handle non-finite values.
Results may differ from a plain program's by a relative error of at most 0.0003.
Values sent between devices are 32-bit elements; how exact they have to be, the bound alone decides.
No kernel may reach another device: no remote copies, remote signals or barrier semaphores. Data moves between devices by JAX's collectives and lax.ppermute only.
A program may use at most 128 MiB of HBM per device.

v0:
```python
import jax
import jax.numpy as jnp
from jax import lax
from jax.sharding import PartitionSpec as P


def orthonormal(image, norms):
    lower = jnp.linalg.cholesky(norms)
    return jax.scipy.linalg.solve_triangular(lower, image.T, lower=True).T


def local(field, basis_species, basis_x, basis_y):
    high = lax.Precision.HIGHEST
    regrouped = lax.all_to_all(field, "sa", split_axis=3, concat_axis=0, tiled=True)
    species = regrouped.shape[0]
    planes = regrouped.shape[1]
    cells_x = regrouped.shape[2]
    cols_y = regrouped.shape[3]
    flat = regrouped.reshape(species, -1)
    gram_species = lax.psum(jnp.dot(flat, flat.T, precision=high), ("gx", "gy", "sa"))
    image_s = jnp.dot(gram_species, basis_species, precision=high)
    factor_species = orthonormal(image_s, jnp.dot(image_s.T, image_s, precision=high))
    rank_s = factor_species.shape[1]
    first = jnp.einsum("spxy,sr->xrpy", regrouped, factor_species, precision=high).reshape(
        cells_x, -1
    )
    pieces = (
        lax.all_gather(first, "gx", axis=0, tiled=True),
        lax.all_gather(basis_x, "gx", axis=0, tiled=True),
    )
    block = jnp.dot(first, pieces[0].T, precision=high)
    partial_x = jnp.dot(block, pieces[1], precision=high)
    image_x = lax.psum(partial_x, ("gy", "sa"))
    norms_x = lax.psum(jnp.dot(image_x.T, image_x, precision=high), "gx")
    factor_x = orthonormal(image_x, norms_x)
    columns = factor_x
    second = lax.psum_scatter(
        jnp.dot(columns.T, first, precision=high), "gx", scatter_dimension=0, tiled=True
    )
    rows_q = second.shape[0]
    mode_y = (
        second.reshape(rows_q, rank_s, planes, cols_y).transpose(3, 0, 1, 2).reshape(cols_y, -1)
    )
    pieces = (
        lax.all_gather(mode_y, ("gy", "sa"), axis=0, tiled=True),
        lax.all_gather(basis_y, ("gy", "sa"), axis=0, tiled=True),
    )
    block = jnp.dot(mode_y, pieces[0].T, precision=high)
    partial_y = jnp.dot(block, pieces[1], precision=high)
    image_y = lax.psum(partial_y, "gx")
    norms_y = lax.psum(jnp.dot(image_y.T, image_y, precision=high), ("gy", "sa"))
    factor_y = orthonormal(image_y, norms_y)
    columns = factor_y
    third = lax.psum_scatter(
        jnp.dot(columns.T, mode_y, precision=high), ("gy", "sa"), scatter_dimension=0, tiled=True
    )
    core = third.reshape(third.shape[0], rows_q, rank_s, planes)
    return (core, factor_species, factor_x, factor_y)


def solution(mesh):
    placed = (P("sa", None, "gx", "gy"), P(), P("gx", None), P(("gy", "sa"), None))
    return jax.shard_map(
        local,
        mesh=mesh,
        in_specs=placed,
        out_specs=(P(("gy", "sa"), "gx", None, None), P(), P("gx", None), P(("gy", "sa"), None)),
        check_vma=False,
    )
```

profile of v0, /device:TPU:0, one launch (start us, length us, event | category | flops | bytes accessed | tf_op | source)
XLA Modules:
  0.0 1318.2 jit_solution(11428051395374100994)
XLA Ops:
  7.2 10.3 copy.45
  17.5 76.7 %all_to_all.18 = f32[12,2,256,256]{2,1,0,3:T(2,128)S(1)} all-to-all(f32[12,2,256,256]{2,1,0,3:T(2,128)} %copy.45), channel_id=1, replica_groups=mesh['gx'=8,'gy'=4,'sa'=4] {'sa'}, dimensions={3} | all-to-all | bytes 12582912 | tf_op jit(solution)/shard_map/all_to_all | solution.py:14
  114.4 9.9 reshape.57
  132.4 65.3 %psum.35 = f32[48,48]{1,0:T(8,128)S(1)} all-reduce(f32[48,48]{1,0:T(8,128)S(1)} %fusion.38), channel_id=1, replica_groups=mesh['gx'=8,'gy'=4,'sa'=4] {'gx','gy','sa'}, use_global_device_ids=true, to_apply=%region_0.0 | all-reduce | flops 2304 | bytes 18432 | tf_op jit(solution)/shard_map/psum | solution.py:20
  203.7 9.6 fusion.2
  217.1 244.6 %all-gather.5.cloned.1.call-done = f32[2048,3072]{0,1:T(8,128)} async-done(((f32[256,3072]{0,1:T(8,128)}), f32[2048,3072]{0,1:T(8,128)}) %all-gather.5.cloned.1.call-update) | async-done | bytes 25165840 | tf_op jit(solution)/shard_map/all_gather | solution.py:28
  461.7 27.0 %fusion.41 = f32[256,2048]{1,0:T(8,128)} fusion(f32[256,3072]{0,1:T(8,128)S(1)} %bitcast.118, f32[2048,3072]{0,1:T(8,128)} %all-gather.5.cloned.1.call-done), kind=kOutput, calls=%fused_computation.79 | convolution fusion | flops 19327352832 | bytes 30408704 | tf_op jit(solution)/shard_map/dot_general | solution.py:31
  488.7 15.1 %all-gather.7.cloned.1.call-done = f32[2048,256]{1,0:T(8,128)} async-done(((f32[256,256]{1,0:T(8,128)}), f32[2048,256]{1,0:T(8,128)}) %all-gather.7.cloned.1.call-update) | async-done | bytes 2097168 | tf_op jit(solution)/shard_map/all_gather | solution.py:29
  508.7 138.0 %all-reduce.6.cloned.1.call-done = f32[256,256]{1,0:T(8,128)} async-done(((f32[256,256]{1,0:T(8,128)}), f32[256,256]{1,0:T(8,128)}) %all-reduce.6.cloned.1.call-update) | async-done | bytes 262160 | tf_op jit(solution)/shard_map/psum | solution.py:33
  649.5 74.7 %all-reduce.8.cloned.1.call-done = f32[256,256]{0,1:T(8,128)} async-done(((f32[256,256]{0,1:T(8,128)}), f32[256,256]{0,1:T(8,128)}) %all-reduce.8.cloned.1.call-update) | async-done | bytes 262160 | tf_op jit(solution)/shard_map/psum | solution.py:34
  727.0 11.7 cholesky.165
  738.8 9.8 custom-call.27
  750.8 11.7 cholesky.182
  769.8 20.3 %custom-call.24 = f32[2,128,128]{1,2,0:T(8,128)} custom-call(f32[2,128,128]{2,1,0:T(8,128)S(1)} %get-tuple-element.12), custom_call_target="InvertDiagBlocksLowerTriangular" | custom-call | tf_op jit(solution)/shard_map/jit(_solve_triangular)/triangular_solve | solution.py:9
  798.4 45.6 %reduce-scatter.3.cloned.1.call-done = f32[32,3072]{1,0:T(8,128)} async-done(((f32[256,3072]{1,0:T(8,128)}), f32[32,3072]{1,0:T(8,128)}) %reduce-scatter.3.cloned.1.call-update) | async-done | bytes 393232 | tf_op jit(solution)/shard_map/reduce_scatter | solution.py:37
  847.4 63.4 %all-gather.9.cloned.1.call-done = f32[1024,1536]{1,0:T(8,128)} async-done(((f32[64,1536]{1,0:T(8,128)}), f32[1024,1536]{1,0:T(8,128)}) %all-gather.9.cloned.1.call-update) | async-done | bytes 6291472 | tf_op jit(solution)/shard_map/all_gather | solution.py:45
  918.6 37.4 %all-gather.11.cloned.1.call-done = f32[1024,256]{1,0:T(8,128)} async-done(((f32[64,256]{1,0:T(8,128)}), f32[1024,256]{1,0:T(8,128)}) %all-gather.11.cloned.1.call-update) | async-done | bytes 1048592 | tf_op jit(solution)/shard_map/all_gather | solution.py:46
  958.6 71.9 %all-reduce.10.cloned.1.call-done = f32[64,256]{1,0:T(8,128)} async-done(((f32[64,256]{1,0:T(8,128)}), f32[64,256]{1,0:T(8,128)}) %all-reduce.10.cloned.1.call-update) | async-done | bytes 65552 | tf_op jit(solution)/shard_map/psum | solution.py:50
  1032.8 139.0 %all-reduce.12.cloned.1.call-done = f32[256,256]{0,1:T(8,128)} async-done(((f32[256,256]{0,1:T(8,128)}), f32[256,256]{0,1:T(8,128)}) %all-reduce.12.cloned.1.call-update) | async-done | bytes 262160 | tf_op jit(solution)/shard_map/psum | solution.py:51
  1173.9 11.7 cholesky.199
  1185.6 9.8 custom-call.28
  1195.9 11.7 cholesky.216
  1214.6 19.7 %custom-call.25 = f32[2,128,128]{1,2,0:T(8,128)S(1)} custom-call(f32[2,128,128]{2,1,0:T(8,128)S(1)} %get-tuple-element.20), custom_call_target="InvertDiagBlocksLowerTriangular" | custom-call | tf_op jit(solution)/shard_map/jit(_solve_triangular)/triangular_solve | solution.py:9
  1240.5 68.3 %reduce-scatter.5.cloned.1.call-done = f32[16,1536]{1,0:T(8,128)} async-done(((f32[256,1536]{1,0:T(8,128)}), f32[16,1536]{1,0:T(8,128)}) %reduce-scatter.5.cloned.1.call-update) | async-done | bytes 98320 | tf_op jit(solution)/shard_map/reduce_scatter | solution.py:54
  (106 shorter events, 105.6 us)
Async XLA Ops:
  7.2 190.5 %copy-start = (f32[48,24]{0,1:T(8,128)S(1)}, f32[48,24]{0,1:T(8,128)}, u32[]{:S(2)}) copy-start(f32[48,24]{0,1:T(8,128)} %param.6) | copy-start | bytes 13828
  7.2 454.5 %all-gather.5.cloned.1.call-start = ((), (), s32[]{:S(2)}) async-start(), calls=%async_computation.3 | async-start | bytes 28311552 | tf_op jit(solution)/shard_map/all_gather | solution.py:28
  203.7 12.4 copy-start.5
  216.1 245.6 %copy-start.2 = (f32[256,24,2,64]{0,3,2,1:T(8,128)S(1)}, f32[256,24,2,64]{0,3,2,1:T(8,128)}, u32[]{:S(2)}) copy-start(f32[256,24,2,64]{0,3,2,1:T(8,128)} %copy.51) | copy-start | bytes 9437188
  216.1 287.7 %all-gather.7.cloned.1.call-start = ((), (), s32[]{:S(2)}) async-start(), calls=%async_computation.4 | async-start | bytes 2359296 | tf_op jit(solution)/shard_map/all_gather | solution.py:29
  216.8 429.9 %all-reduce.6.cloned.1.call-start = ((), (), s32[]{:S(2)}) async-start(), calls=%async_computation.5 | async-start | bytes 524288 | tf_op jit(solution)/shard_map/psum | solution.py:33
  508.7 215.6 %all-reduce.8.cloned.1.call-start = ((), (), s32[]{:S(2)}) async-start(), calls=%async_computation.6 | async-start | bytes 524288 | tf_op jit(solution)/shard_map/psum | solution.py:34
  649.1 195.0 %reduce-scatter.3.cloned.1.call-start = ((), (), s32[]{:S(2)}) async-start(), calls=%async_computation.7 | async-start | bytes 3538944 | tf_op jit(solution)/shard_map/reduce_scatter | solution.py:37
  726.3 0.7 copy-start.4
  762.5 2.0 copy-start.3
  798.3 112.5 %all-gather.9.cloned.1.call-start = ((), (), s32[]{:S(2)}) async-start(), calls=%async_computation.8 | async-start | bytes 6684672 | tf_op jit(solution)/shard_map/all_gather | solution.py:45
  846.6 109.4 %all-gather.11.cloned.1.call-start = ((), (), s32[]{:S(2)}) async-start(), calls=%async_computation.9 | async-start | bytes 1114112 | tf_op jit(solution)/shard_map/all_gather | solution.py:46
  847.4 183.1 %all-reduce.10.cloned.1.call-start = ((), (), s32[]{:S(2)}) async-start(), calls=%async_computation.10 | async-start | bytes 131072 | tf_op jit(solution)/shard_map/psum | solution.py:50
  956.0 355.1 %copy-start.1 = (f32[48,24]{0,1:T(8,128)S(1)}, f32[48,24]{0,1:T(8,128)}, u32[]{:S(2)}) copy-start(f32[48,24]{0,1:T(8,128)} %param.6) | copy-start | bytes 13828
  958.5 213.2 %all-reduce.12.cloned.1.call-start = ((), (), s32[]{:S(2)}) async-start(), calls=%async_computation.11 | async-start | bytes 524288 | tf_op jit(solution)/shard_map/psum | solution.py:51
  1032.5 276.3 %reduce-scatter.5.cloned.1.call-start = ((), (), s32[]{:S(2)}) async-start(), calls=%async_computation.12 | async-start | bytes 1671168 | tf_op jit(solution)/shard_map/reduce_scatter | solution.py:54
Sparse Core Ops, SparseCore 0:
  216.2 245.4 all-gather.4
  463.3 40.4 all-gather.6
  508.8 137.8 all-reduce.5
  649.7 74.4 all-reduce.7
  798.5 45.5 reduce-scatter.2
  846.9 63.8 all-gather.8
  913.3 42.6 all-gather.10
  959.0 71.4 all-reduce.9
  1033.7 138.0 all-reduce.11
  1239.2 69.5 reduce-scatter.4
where the time goes:
time: 1320 us
  waiting for transfers between devices  899 us (68%)
  blocking collectives  142 us (11%)
  other arithmetic  118 us (9%)
  matrix products  80.3 us (6%)
  local copies, waits for them, and re-layouts  59.7 us (5%)
  between operations  17.3 us (1%)
    all_gather x1, waiting for transfers between devices, local(): lax.all_gather(first, 'gx', axis=0, tiled=True)  245 us
    psum x1, waiting for transfers between devices, local(): lax.psum(jnp.dot(image_y.T, image_y, precision=high), ('gy', 'sa'))  139 us
    psum x1, waiting for transfers between devices, local(): image_x = lax.psum(partial_x, ('gy', 'sa'))  138 us
    all_to_all x1, blocking collectives, local(): lax.all_to_all(field, 'sa', split_axis=3, concat_axis=0, tiled=True)  76.7 us
    psum x1, waiting for transfers between devices, local(): norms_x = lax.psum(jnp.dot(image_x.T, image_x, precision=high), 'gx')  74.7 us
    psum x1, waiting for transfers between devices, local(): image_y = lax.psum(partial_y, 'gx')  71.9 us
    another operation x16, other arithmetic, orthonormal(): lower = jnp.linalg.cholesky(norms)  71.5 us
    reduce_scatter x1, waiting for transfers between devices, local(): lax.psum_scatter(jnp.dot(columns.T, mode_y, precision=high), ('gy', 'sa')...  68.3 us
  transfers between devices with their start and end apart: 10, of which 10 were waited for; matrix products, arithmetic and copies ran while one was open for 3% of the time, Pallas kernels for 0%

commit v1 on v0

v1 whole, which is shorter than its diff:
```python
import functools

import jax
import jax.numpy as jnp
from jax import lax
from jax.experimental import pallas as pl
from jax.experimental.pallas import tpu as pltpu
from jax.sharding import Mesh
from jax.sharding import PartitionSpec as P

F32 = jnp.float32
BF16 = jnp.bfloat16
HIGH = lax.Precision.HIGHEST
GX = ("xl", "y")
GY = ("xh", "c")
VMEM = pl.BlockSpec(memory_space=pltpu.VMEM)
SMEM = pl.BlockSpec(memory_space=pltpu.SMEM)
PARAMS = pltpu.CompilerParams(vmem_limit_bytes=48 * 1024 * 1024)

NN = (((1,), (0,)), ((), ()))
NT = (((1,), (1,)), ((), ()))
TN = (((0,), (0,)), ((), ()))


def exact(a, b, dims=NN):
    return lax.dot_general(a, b, dims, precision=HIGH, preferred_element_type=F32)


def split(a):
    hi = a.astype(BF16)
    return hi, (a - hi.astype(F32)).astype(BF16)


def dot3(a, b, dims=NN):
    one = functools.partial(lax.dot_general, dimension_numbers=dims, preferred_element_type=F32)
    return one(a[0], b[0]) + (one(a[0], b[1]) + one(a[1], b[0]))


def iota(shape, dim):
    return lax.broadcasted_iota(jnp.int32, shape, dim)


def invert_block(block):
    n = block.shape[0]
    unit = (iota((n, n), 0) == iota((n, n), 1)).astype(F32)
    work = jnp.concatenate([block, unit], axis=1)
    rows = []
    for j in range(n):
        base = (j // 8) * 8
        local = j - base
        pivot = work[local : local + 1, :]
        scaled = pivot * (1.0 / pivot[:, j : j + 1])
        rows.append(pivot[:, n:] * lax.rsqrt(pivot[:, j : j + 1]))
        if j + 1 < n:
            if local == 7:
                work = work[8:, :]
            work = work - work[:, j : j + 1] * scaled
    return jnp.concatenate(rows, axis=0)


def invert_factor(work_ref, n, size):
    for k in range(0, n, size):
        inner = invert_block(work_ref[k : k + size, k : k + size])
        row = exact(inner, work_ref[k : k + size, :])
        work_ref[k : k + size, :] = row
        if k + size < n:
            work_ref[k + size :, :] -= exact(row[:, k + size : n], row, TN)
    return work_ref[:, n:]


def fill(work_ref, norms):
    n = norms.shape[0]
    work_ref[:, :n] = norms
    work_ref[:, n:] = (iota((n, n), 0) == iota((n, n), 1)).astype(F32)


def pack_kernel(field_ref, out_ref):
    planes = field_ref.shape[1]
    for p in range(planes):
        turned = field_ref[0, p].T
        out_ref[:, 0, p] = turned.reshape(out_ref.shape[0], 8, turned.shape[1])


def pack(field, groups):
    species, planes, rows, cols = field.shape
    return pl.pallas_call(
        pack_kernel,
        grid=(species,),
        in_specs=[pl.BlockSpec((1, planes, rows, cols), lambda s: (s, 0, 0, 0))],
        out_specs=pl.BlockSpec((groups, 1, planes, 8, rows), lambda s: (0, s, 0, 0, 0)),
        out_shape=jax.ShapeDtypeStruct((groups, species, planes, 8, rows), F32),
        compiler_params=PARAMS,
        name="pack",
    )(field)


def gram_kernel(cells_ref, out_ref, acc_ref):
    step = pl.program_id(0) * pl.num_programs(1) + pl.program_id(1)

    @pl.when(step == 0)
    def _():
        acc_ref[...] = jnp.zeros_like(acc_ref)

    count = acc_ref.shape[0]
    cells = cells_ref[...].reshape(count, cells_ref.shape[-1])
    hi, lo = split(cells)
    twice = (lo.astype(F32) * 2.0).astype(BF16)
    one = functools.partial(lax.dot_general, dimension_numbers=NT, preferred_element_type=F32)
    acc_ref[...] += one(hi, hi) + one(hi, twice)

    @pl.when(step == pl.num_programs(0) * pl.num_programs(1) - 1)
    def _():
        same = (iota((count, count), 0) % 8) == (iota((count, count), 1) % 8)
        kept = jnp.where(same, acc_ref[...], 0.0)
        pick = (iota((count, 128), 0) // 8 == iota((count, 128), 1)).astype(F32)
        summed = exact(exact(pick, kept, TN), pick)
        both = 0.5 * (summed + summed.T)
        out_ref[...] = both[: out_ref.shape[0], :]


def gram(cells):
    sa, gx, own, planes, eight, width = cells.shape
    species = sa * own
    return pl.pallas_call(
        gram_kernel,
        grid=(gx, planes),
        in_specs=[pl.BlockSpec((sa, 1, own, 1, eight, width), lambda g, p: (0, g, 0, p, 0, 0))],
        out_specs=pl.BlockSpec((species, 128), lambda g, p: (0, 0)),
        out_shape=jax.ShapeDtypeStruct((species, 128), F32),
        scratch_shapes=[pltpu.VMEM((species * 8, species * 8), F32)],
        compiler_params=PARAMS,
        name="gram_species",
    )(cells)


def first_kernel(grams_ref, basis_s_ref, basis_x_ref, cells_ref, factor_ref, first_ref, image_ref, hold_ref):
    sa, gx, own, planes, eight, width = cells_ref.shape
    species, rank = basis_s_ref.shape
    gram_all = jnp.sum(grams_ref[...], axis=0)[:, :species]
    image = exact(gram_all, basis_s_ref[...])
    norms = exact(image, image, TN)
    factor = exact(image, invert_block(norms), NT)
    factor_ref[...] = factor
    low, wide = rank * 8, species * 8
    rep_r = (iota((low, rank), 0) // 8 == iota((low, rank), 1)).astype(F32)
    rep_s = (iota((species, wide), 0) == iota((species, wide), 1) // 8).astype(F32)
    mixed = exact(exact(rep_r, factor, NT), rep_s)
    same = (iota((low, wide), 0) % 8) == (iota((low, wide), 1) % 8)
    mix = split(jnp.where(same, mixed, 0.0))
    hold_ref[...] = jnp.zeros_like(hold_ref)

    @pl.loop(0, gx)
    def _(g):
        basis = split(basis_x_ref[g])
        for p in range(planes):
            cells = split(cells_ref[:, g, :, p].reshape(wide, width))
            first = dot3(mix, cells)
            first_ref[g, p * low : (p + 1) * low, :] = first
            hold_ref[p * low : (p + 1) * low, :] += dot3(split(first), basis)

    turned = split(hold_ref[...].T)

    @pl.loop(0, gx)
    def _(g):
        image_ref[g] = dot3(turned, split(first_ref[g]))


def first_stage(grams, basis_s, basis_x, cells):
    sa, gx, own, planes, eight, width = cells.shape
    species, rank = basis_s.shape
    low = rank * 8
    return pl.pallas_call(
        first_kernel,
        in_specs=[VMEM] * 4,
        out_specs=[VMEM] * 3,
        out_shape=[
            jax.ShapeDtypeStruct((species, rank), F32),
            jax.ShapeDtypeStruct((gx, planes * low, width), F32),
            jax.ShapeDtypeStruct((gx, basis_x.shape[2], width), F32),
        ],
        scratch_shapes=[pltpu.VMEM((planes * low, basis_x.shape[2]), F32)],
        compiler_params=PARAMS,
        name="first_and_image_x",
    )(grams, basis_s, basis_x, cells)


def second_kernel(place_ref, image_ref, first_ref, factor_ref, send_ref, work_ref, hold_ref):
    gx, rank, width = image_ref.shape
    n = rank
    work_ref[...] = jnp.zeros_like(work_ref)
    hold_ref[...] = jnp.zeros_like(hold_ref)

    @pl.loop(0, gx)
    def _(g):
        image = image_ref[g]
        both = split(image)
        work_ref[:, :n] += exact(image, image, NT)
        hold_ref[...] += dot3(split(first_ref[g]), both, NT)

    work_ref[:, n:] = (iota((n, n), 0) == iota((n, n), 1)).astype(F32)
    inverse = invert_factor(work_ref, n, 64)
    factor_ref[...] = exact(inverse, image_ref[place_ref[0]]).T
    second = exact(hold_ref[...], inverse, NT)
    hold_ref[...] = second
    groups = send_ref.shape[0] // gx
    each = 3
    lane = iota((8, 128), 1)
    for g in range(groups):
        for half in range(n // 128):
            tiles = [
                hold_ref[(g * each + j) * 8 : (g * each + j + 1) * 8, half * 128 : (half + 1) * 128]
                for j in range(each)
            ]
            for part in range(4):
                moved = [
                    tile if (j - part) % 4 == 0 else pltpu.roll(tile, ((j - part) % 4) * 32, 1)
                    for j, tile in enumerate(tiles)
                ]
                mixed = jnp.where(lane < 32, moved[0], jnp.where(lane < 64, moved[1], moved[2]))
                send_ref[g * gx + half * 4 + part] = jnp.where(lane < 96, mixed, 0.0)


def second_stage(place, image, first):
    gx, rank, width = image.shape
    rows = first.shape[1]
    return pl.pallas_call(
        second_kernel,
        in_specs=[SMEM, VMEM, VMEM],
        out_specs=[VMEM] * 2,
        out_shape=[
            jax.ShapeDtypeStruct((width, rank), F32),
            jax.ShapeDtypeStruct((rows // 24 * gx, 8, 128), F32),
        ],
        scratch_shapes=[pltpu.VMEM((rank, 2 * rank), F32), pltpu.VMEM((rows, rank), F32)],
        compiler_params=PARAMS,
        name="factor_x_and_second",
    )(place, image, first)


def image_y_kernel(second_ref, basis_ref, image_ref):
    turned = second_ref[...].T
    both = split(turned)
    inner = dot3(both, split(basis_ref[...]))
    left = split(inner.T)
    blocks, rank, width = image_ref.shape
    for b in range(blocks):
        cols = slice(b * width, (b + 1) * width)
        image_ref[b] = dot3(left, (both[0][:, cols], both[1][:, cols]))


def image_y_stage(second, basis_y):
    rows, rank = basis_y.shape
    return pl.pallas_call(
        image_y_kernel,
        in_specs=[VMEM] * 2,
        out_specs=VMEM,
        out_shape=jax.ShapeDtypeStruct((rows // 256, rank, 256), F32),
        compiler_params=PARAMS,
        name="image_y",
    )(second, basis_y)


def core_kernel(place_ref, image_ref, second_ref, factor_ref, core_ref, work_ref, turn_ref):
    blocks, n, width = image_ref.shape
    norms = jnp.zeros((n, n), F32)
    raw = jnp.zeros((n, second_ref.shape[1]), F32)
    for b in range(blocks):
        image = image_ref[b]
        norms += exact(image, image, NT)
        raw += exact(image, second_ref[b * width : (b + 1) * width, :])
    fill(work_ref, norms)
    inverse = invert_factor(work_ref, n, 64)
    core_ref[...] = exact(inverse, raw)
    turn_ref[...] = exact(inverse, image_ref[place_ref[0]]).T
    count = factor_ref.shape[0]
    factor_ref[...] = turn_ref[pl.ds(pl.multiple_of(place_ref[1] * count, count), count), :]


def core_stage(place, image, second, count):
    blocks, n, width = image.shape
    return pl.pallas_call(
        core_kernel,
        in_specs=[SMEM, VMEM, VMEM],
        out_specs=[VMEM] * 2,
        out_shape=[
            jax.ShapeDtypeStruct((count, n), F32),
            jax.ShapeDtypeStruct((n, second.shape[1]), F32),
        ],
        scratch_shapes=[pltpu.VMEM((n, 2 * n), F32), pltpu.VMEM((width, n), F32)],
        compiler_params=PARAMS,
        name="factor_y_and_core",
    )(place, image, second)


def swap(parts, axes):
    return lax.all_to_all(parts, axes, split_axis=0, concat_axis=0, tiled=True)


def spread(one, axes, count):
    return swap(jnp.broadcast_to(one, (count,) + one.shape), axes)


def total(partial):
    chips = GX + ("xh", "z")
    size = partial.size // 256
    mine = jnp.sum(swap(partial.reshape(2, size // 2, 256), "c"), axis=0)
    mine = jnp.sum(swap(mine.reshape(64, size // 128, 256), chips), axis=0)
    half = spread(mine, chips, 64)
    return spread(half, "c", 2).reshape(partial.shape)


def local(field, basis_s, basis_x, basis_y):
    gx_n, sa_n = 8, 4
    basis_x_all = lax.all_gather(basis_x, GX, axis=0)
    basis_y_all = lax.all_gather(basis_y, GY + ("z",), axis=0, tiled=True)
    cells = swap(pack(field, gx_n * sa_n), ("z",) + GX)
    cells = cells.reshape((sa_n, gx_n) + cells.shape[1:])
    partial = jnp.sum(spread(gram(cells), GX, gx_n), axis=0)
    grams = spread(partial, GY + ("z",), 16)
    factor_s, first, image_part = first_stage(grams, basis_s, basis_x_all, cells)
    image_x = total(image_part)
    gx = lax.axis_index(GX)
    factor_x, send = second_stage(jnp.reshape(gx, (1,)), image_x, first)
    second = swap(send, GY + ("z",) + GX).reshape(-1, 128)
    image_y = total(image_y_stage(second, basis_y_all))
    place = jnp.stack([lax.axis_index(GY), lax.axis_index("z")])
    factor_y, core = core_stage(place, image_y, second, basis_y.shape[0])
    rank_y = core.shape[0]
    blocks = swap(core.reshape(16, rank_y // 16, 128), GY + ("z",))
    core = blocks.reshape(2, 8, rank_y // 16, 4, 32)[:, :, :, :3, :]
    core = core.transpose(2, 4, 1, 3, 0).reshape(rank_y // 16, 32, 24, 2)
    return core, factor_s, factor_x, factor_y


def solution(mesh):
    fine = Mesh(mesh.devices.reshape(2, 4, 2, 2, 4), ("xl", "y", "xh", "c", "z"))
    yz = GY + ("z",)
    return jax.shard_map(
        local,
        mesh=fine,
        in_specs=(P("z", None, GX, GY), P(), P(GX, None), P(yz, None)),
        out_specs=(P(yz, GX, None, None), P(), P(GX, None), P(yz, None)),
        check_vma=False,
    )
```

time: 1320 us -> 404 us (0.31)
  waiting for transfers between devices: 899 us -> 173 us
  other arithmetic: 118 us -> 1.65 us
  Pallas kernels: 0 us -> 103 us
  matrix products: 80.3 us -> 0 us
  blocking collectives: 142 us -> 61.9 us
  local copies, waits for them, and re-layouts: 59.7 us -> 7.99 us
  starting transfers between devices: 1.24 us -> 39.7 us
    psum x4 -> x0, waiting for transfers between devices: 424 us -> none  [the longest x1 139 us: local(): lax.psum(jnp.dot(image_y.T, image_y, precision=high), ('gy', 'sa'))]
    all_gather x4 -> x2, waiting for transfers between devices: 361 us -> 0.03 us  [the longest x1 0.03 us: local(): basis_y_all = lax.all_gather(basis_y, GY + ('z',), axis=0, tiled=True)]
    all_to_all x0 -> x7, waiting for transfers between devices: none -> 171 us  [swap(): return lax.all_to_all(parts, axes, split_axis=0, concat_axis=0, tiled=True)]
    another operation x23 -> x1, other arithmetic: 115 us -> 0.08 us  [local(): place = jnp.stack([lax.axis_index(GY), lax.axis_index('z')])]
    reduce_scatter x2 -> x0, waiting for transfers between devices: 114 us -> none  [the longest x1 68.3 us: local(): lax.psum_scatter(jnp.dot(columns.T, mode_y, precision=high), ('gy', 'sa')...]
    pallas_call x0 -> x6, Pallas kernels: none -> 103 us  [the longest x1 30.4 us: second_stage(): pl.pallas_call(second_kernel, in_specs=[SMEM, VMEM, VMEM], out_specs=[VME...]
    dot_general x12 -> x0, matrix products: 71.7 us -> none  [the longest x1 27 us: local(): block = jnp.dot(first, pieces[0].T, precision=high)]
    psum x1 -> x0, blocking collectives: 65.3 us -> none  [local(): lax.psum(jnp.dot(flat, flat.T, precision=high), ('gx', 'gy', 'sa'))]
  transfers between devices with their start and end apart: 10 -> 9, of which waited for: 10 -> 7; matrix products, arithmetic and copies ran while one was open for 3% -> 1% of each run, Pallas kernels for 0% -> 11%
where the time goes in v1:
time: 404 us; the launch traced here: 402 us
  waiting for transfers between devices  173 us (43%)
  Pallas kernels  103 us (25%)
  blocking collectives  61.9 us (15%)
  starting transfers between devices  39.7 us (10%)
  between operations  15.6 us (4%)
  local copies, waits for them, and re-layouts  7.99 us (2%)
    all_to_all x7, waiting for transfers between devices, swap(): return lax.all_to_all(parts, axes, split_axis=0, concat_axis=0, tiled=True)  171 us
    all_to_all x6, blocking collectives, swap(): return lax.all_to_all(parts, axes, split_axis=0, concat_axis=0, tiled=True)  61.9 us
    all_to_all x7, starting transfers between devices, swap(): return lax.all_to_all(parts, axes, split_axis=0, concat_axis=0, tiled=True)  39.6 us
    pallas_call x1, Pallas kernels, second_stage(): pl.pallas_call(second_kernel, in_specs=[SMEM, VMEM, VMEM], out_specs=[VME...  30.4 us
    pallas_call x1, Pallas kernels, core_stage(): pl.pallas_call(core_kernel, in_specs=[SMEM, VMEM, VMEM], out_specs=[VMEM]...  27.3 us
    pallas_call x1, Pallas kernels, first_stage(): pl.pallas_call(first_kernel, in_specs=[VMEM] * 4, out_specs=[VMEM] * 3, o...  20.1 us
    pallas_call x1, Pallas kernels, gram(): pl.pallas_call(gram_kernel, grid=(gx, planes), in_specs=[pl.BlockSpec((sa...  13.1 us
    pallas_call x1, Pallas kernels, pack(): pl.pallas_call(pack_kernel, grid=(species,), in_specs=[pl.BlockSpec((1, p...  10.3 us
  transfers between devices with their start and end apart: 9, of which 7 were waited for; matrix products, arithmetic and copies ran while one was open for 1% of the time, Pallas kernels for 11%

profile of v1, /device:TPU:0, one launch (start us, length us, event | category | flops | bytes accessed | tf_op | source)
XLA Modules:
  0.0 402.0 jit_solution(7491993566480342052)
XLA Ops:
  8.0 10.3 %pack.1 = f32[32,12,2,8,256]{4,3,2,1,0:T(8,128)} custom-call(f32[12,2,256,256]{3,2,1,0:T(8,128)} %field_ref.1), custom_call_target="tpu_custom_call" | custom-call | tf_op jit(solution)/shard_map/pack/pallas_call | solution.py:86
  18.3 9.5 %all-to-all-start = ((f32[32,12,2,8,256]{4,3,2,1,0:T(8,128)}), f32[32,12,2,8,256]{4,3,2,1,0:T(8,128)}, u32[]{:S(2)}, u32[]{:S(2)}) async-start(f32[32,12,2,8,256]{4,3,2,1,0:T(8,128)} %pack.1), calls=%async_computation | async-start | bytes 12582912 | tf_op jit(solution)/shard_map/all_to_all | solution.py:296
  28.5 91.8 %all-to-all-done = f32[32,12,2,8,256]{4,3,2,1,0:T(8,128)} async-done(((f32[32,12,2,8,256]{4,3,2,1,0:T(8,128)}), f32[32,12,2,8,256]{4,3,2,1,0:T(8,128)}, u32[]{:S(2)}, u32[]{:S(2)}) %all-to-all-start) | async-done | bytes 6291488 | tf_op jit(solution)/shard_map/all_to_all | solution.py:296
  120.2 13.1 %gram_species.1 = f32[48,128]{1,0:T(8,128)S(1)} custom-call(f32[4,8,12,2,8,256]{5,4,3,2,1,0:T(8,128)} %bitcast.3.cells_ref), custom_call_target="tpu_custom_call" | custom-call | tf_op jit(solution)/shard_map/gram_species/pallas_call | solution.py:124
  133.4 23.3 %all_to_all.65 = f32[8,48,128]{2,1,0:T(8,128)S(1)} all-to-all(f32[8,48,128]{2,1,0:T(8,128)S(1)} %broadcast_in_dim.18), channel_id=1, replica_groups=mesh['xl'=2,'y'=4,'xh'=2,'c'=2,'z'=4] {'xl','y'}, dimensions={0} | all-to-all | bytes 393216 | tf_op jit(solution)/shard_map/all_to_all | solution.py:296
  157.5 4.7 %all-to-all-start.2 = ((f32[16,48,128]{2,1,0:T(8,128)}), f32[16,48,128]{2,1,0:T(8,128)S(1)}, u32[]{:S(2)}, u32[]{:S(2)}) async-start(f32[16,48,128]{2,1,0:T(8,128)} %broadcast_in_dim.19), calls=%async_computation.2 | async-start | bytes 786432 | tf_op jit(solution)/shard_map/all_to_all | solution.py:296
  162.3 10.8 %all-to-all-done.2.grams_ref = f32[16,48,128]{2,1,0:T(8,128)S(1)} async-done(((f32[16,48,128]{2,1,0:T(8,128)}), f32[16,48,128]{2,1,0:T(8,128)S(1)}, u32[]{:S(2)}, u32[]{:S(2)}) %all-to-all-start.2) | async-done | bytes 393248 | tf_op jit(solution)/shard_map/all_to_all | solution.py:296
  174.7 20.1 %first_and_image_x.1 = (f32[48,24]{1,0:T(8,128)S(1)}, f32[8,384,256]{2,1,0:T(8,128)}, f32[8,256,256]{2,1,0:T(8,128)S(1)}) custom-call(f32[16,48,128]{2,1,0:T(8,128)S(1)} %all-to-all-done.2.grams_ref, f32[48,24]{1,0:T(8,128)S(1)} %copy.11.basis_s_ref, f32[8,256,256]{2,1,0:T(8,128)S(1)} %bitcast.22, f32[4,8,12,2,8,256]{5,4,3,2,1,0:T(8,128)} %bitcast.3.cells_ref), custom_call_target="tpu_custom_call" | custom-call | tf_op jit(solution)/shard_map/first_and_image_x/pallas_call | solution.py:172
  194.8 5.4 %all_to_all.66 = f32[2,1024,256]{2,1,0:T(8,128)S(1)} all-to-all(f32[2,1024,256]{2,1,0:T(8,128)S(1)} %bitcast.23), channel_id=1, replica_groups=mesh['xl'=2,'y'=4,'xh'=2,'c'=2,'z'=4] {'c'}, dimensions={0} | all-to-all | bytes 4194304 | tf_op jit(solution)/shard_map/all_to_all | solution.py:296
  201.4 4.7 %all-to-all-start.4 = ((f32[64,16,256]{2,1,0:T(8,128)}), f32[64,16,256]{2,1,0:T(8,128)S(1)}, u32[]{:S(2)}, u32[]{:S(2)}) async-start(f32[64,16,256]{2,1,0:T(8,128)} %bitcast.6), calls=%async_computation.4 | async-start | bytes 2097152 | tf_op jit(solution)/shard_map/all_to_all | solution.py:296
  206.7 17.9 %all-to-all-done.4 = f32[64,16,256]{2,1,0:T(8,128)S(1)} async-done(((f32[64,16,256]{2,1,0:T(8,128)}), f32[64,16,256]{2,1,0:T(8,128)S(1)}, u32[]{:S(2)}, u32[]{:S(2)}) %all-to-all-start.4) | async-done | bytes 1048608 | tf_op jit(solution)/shard_map/all_to_all | solution.py:296
  225.8 5.8 %all-to-all-start.5 = ((f32[64,16,256]{2,1,0:T(8,128)}), f32[64,16,256]{2,1,0:T(8,128)S(1)}, u32[]{:S(2)}, u32[]{:S(2)}) async-start(f32[64,16,256]{2,1,0:T(8,128)} %broadcast_in_dim.20), calls=%async_computation.5 | async-start | bytes 2097152 | tf_op jit(solution)/shard_map/all_to_all | solution.py:296
  231.6 18.8 %all-to-all-done.5 = f32[64,16,256]{2,1,0:T(8,128)S(1)} async-done(((f32[64,16,256]{2,1,0:T(8,128)}), f32[64,16,256]{2,1,0:T(8,128)S(1)}, u32[]{:S(2)}, u32[]{:S(2)}) %all-to-all-start.5) | async-done | bytes 1048608 | tf_op jit(solution)/shard_map/all_to_all | solution.py:296
  250.7 5.7 %all_to_all.67 = f32[2,64,16,256]{3,2,1,0:T(8,128)S(1)} all-to-all(f32[2,64,16,256]{3,2,1,0:T(8,128)S(1)} %broadcast_in_dim.21), channel_id=1, replica_groups=mesh['xl'=2,'y'=4,'xh'=2,'c'=2,'z'=4] {'c'}, dimensions={0} | all-to-all | bytes 4194304 | tf_op jit(solution)/shard_map/all_to_all | solution.py:296
  256.4 30.4 %factor_x_and_second.1 = (f32[256,256]{1,0:T(8,128)}, f32[128,8,128]{2,1,0:T(8,128)}) custom-call(s32[1]{0:T(128)} %bitcast.2.place_ref, f32[8,256,256]{2,1,0:T(8,128)S(1)} %bitcast.17, f32[8,384,256]{2,1,0:T(8,128)S(1)} %copy-done), custom_call_target="tpu_custom_call" | custom-call | tf_op jit(solution)/shard_map/factor_x_and_second/pallas_call | solution.py:226
  286.8 6.1 %all-to-all-start.7 = ((f32[128,8,128]{2,1,0:T(8,128)}), f32[128,8,128]{2,1,0:T(8,128)S(1)}, u32[]{:S(2)}, u32[]{:S(2)}) async-start(f32[128,8,128]{2,1,0:T(8,128)} %get-tuple-element.13), calls=%async_computation.7 | async-start | bytes 1048576 | tf_op jit(solution)/shard_map/all_to_all | solution.py:296
  292.9 13.3 %all-to-all-done.7 = f32[128,8,128]{2,1,0:T(8,128)S(1)} async-done(((f32[128,8,128]{2,1,0:T(8,128)}), f32[128,8,128]{2,1,0:T(8,128)S(1)}, u32[]{:S(2)}, u32[]{:S(2)}) %all-to-all-start.7) | async-done | bytes 524320 | tf_op jit(solution)/shard_map/all_to_all | solution.py:296
  308.8 4.6 %all_to_all.68 = f32[2,512,256]{2,1,0:T(8,128)S(1)} all-to-all(f32[2,512,256]{2,1,0:T(8,128)S(1)} %bitcast.21), channel_id=1, replica_groups=mesh['xl'=2,'y'=4,'xh'=2,'c'=2,'z'=4] {'c'}, dimensions={0} | all-to-all | bytes 2097152 | tf_op jit(solution)/shard_map/all_to_all | solution.py:296
  313.5 18.3 %all_to_all.69 = f32[64,8,256]{2,1,0:T(8,128)S(1)} all-to-all(f32[64,8,256]{2,1,0:T(8,128)S(1)} %bitcast.25), channel_id=1, replica_groups=mesh['xl'=2,'y'=4,'xh'=2,'c'=2,'z'=4] {'xl','y','xh','z'}, dimensions={0} | all-to-all | bytes 1048576 | tf_op jit(solution)/shard_map/all_to_all | solution.py:296
  332.7 5.2 %all-to-all-start.10 = ((f32[64,8,256]{2,1,0:T(8,128)}), f32[64,8,256]{2,1,0:T(8,128)S(1)}, u32[]{:S(2)}, u32[]{:S(2)}) async-start(f32[64,8,256]{2,1,0:T(8,128)} %broadcast_in_dim.22), calls=%async_computation.10 | async-start | bytes 1048576 | tf_op jit(solution)/shard_map/all_to_all | solution.py:296
  338.0 11.7 %all-to-all-done.10 = f32[64,8,256]{2,1,0:T(8,128)S(1)} async-done(((f32[64,8,256]{2,1,0:T(8,128)}), f32[64,8,256]{2,1,0:T(8,128)S(1)}, u32[]{:S(2)}, u32[]{:S(2)}) %all-to-all-start.10) | async-done | bytes 524320 | tf_op jit(solution)/shard_map/all_to_all | solution.py:296
  349.8 4.6 %all_to_all.70 = f32[2,64,8,256]{3,2,1,0:T(8,128)S(1)} all-to-all(f32[2,64,8,256]{3,2,1,0:T(8,128)S(1)} %broadcast_in_dim.23), channel_id=1, replica_groups=mesh['xl'=2,'y'=4,'xh'=2,'c'=2,'z'=4] {'c'}, dimensions={0} | all-to-all | bytes 2097152 | tf_op jit(solution)/shard_map/all_to_all | solution.py:296
  354.3 27.3 %factor_y_and_core.1 = (f32[64,256]{1,0:T(8,128)}, f32[256,128]{1,0:T(8,128)}) custom-call(s32[2]{0:T(128)S(1)} %pad_add_fusion.place_ref, f32[4,256,256]{2,1,0:T(8,128)S(1)} %bitcast.20, f32[1024,128]{1,0:T(8,128)S(1)} %bitcast.19), custom_call_target="tpu_custom_call" | custom-call | tf_op jit(solution)/shard_map/factor_y_and_core/pallas_call | solution.py:281
  385.9 7.3 %all-to-all-done.12 = f32[16,16,128]{2,1,0:T(8,128)S(1)} async-done(((f32[16,16,128]{2,1,0:T(8,128)}), f32[16,16,128]{2,1,0:T(8,128)S(1)}, u32[]{:S(2)}, u32[]{:S(2)}) %all-to-all-start.12) | async-done | bytes 131104 | tf_op jit(solution)/shard_map/all_to_all | solution.py:296
  (32 shorter events, 16.0 us)
Async XLA Ops:
  18.3 102.0 %all-to-all-start = ((f32[32,12,2,8,256]{4,3,2,1,0:T(8,128)}), f32[32,12,2,8,256]{4,3,2,1,0:T(8,128)}, u32[]{:S(2)}, u32[]{:S(2)}) async-start(f32[32,12,2,8,256]{4,3,2,1,0:T(8,128)} %pack.1), calls=%async_computation | async-start | bytes 12582912 | tf_op jit(solution)/shard_map/all_to_all | solution.py:296
  27.7 134.6 %all-gather.6.cloned.1.call-start = ((), (), s32[]{:S(2)}) async-start(), calls=%async_computation.14 | async-start | bytes 2359296 | tf_op jit(solution)/shard_map/all_gather | solution.py:314
  120.2 42.0 %copy-start.3 = (f32[48,24]{0,1:T(8,128)S(1)}, f32[48,24]{0,1:T(8,128)}, u32[]{:S(2)}) copy-start(f32[48,24]{0,1:T(8,128)} %param.5) | copy-start | bytes 13828
  157.5 15.6 %all-to-all-start.2 = ((f32[16,48,128]{2,1,0:T(8,128)}), f32[16,48,128]{2,1,0:T(8,128)S(1)}, u32[]{:S(2)}, u32[]{:S(2)}) async-start(f32[16,48,128]{2,1,0:T(8,128)} %broadcast_in_dim.19), calls=%async_computation.2 | async-start | bytes 786432 | tf_op jit(solution)/shard_map/all_to_all | solution.py:296
  173.1 1.6 copy-start.1
  201.4 23.1 %all-to-all-start.4 = ((f32[64,16,256]{2,1,0:T(8,128)}), f32[64,16,256]{2,1,0:T(8,128)S(1)}, u32[]{:S(2)}, u32[]{:S(2)}) async-start(f32[64,16,256]{2,1,0:T(8,128)} %bitcast.6), calls=%async_computation.4 | async-start | bytes 2097152 | tf_op jit(solution)/shard_map/all_to_all | solution.py:296
  206.1 86.8 %all-gather.4.cloned.1.call-start = ((), (), s32[]{:S(2)}) async-start(), calls=%async_computation.13 | async-start | bytes 1114112 | tf_op jit(solution)/shard_map/all_gather | solution.py:315
  225.8 24.6 %all-to-all-start.5 = ((f32[64,16,256]{2,1,0:T(8,128)}), f32[64,16,256]{2,1,0:T(8,128)S(1)}, u32[]{:S(2)}, u32[]{:S(2)}) async-start(f32[64,16,256]{2,1,0:T(8,128)} %broadcast_in_dim.20), calls=%async_computation.5 | async-start | bytes 2097152 | tf_op jit(solution)/shard_map/all_to_all | solution.py:296
  250.7 5.7 %copy-start = (f32[8,384,256]{2,1,0:T(8,128)S(1)}, f32[8,384,256]{2,1,0:T(8,128)}, u32[]{:S(2)}) copy-start(f32[8,384,256]{2,1,0:T(8,128)} %get-tuple-element.12.first_ref) | copy-start | bytes 9437188
  286.8 19.4 %all-to-all-start.7 = ((f32[128,8,128]{2,1,0:T(8,128)}), f32[128,8,128]{2,1,0:T(8,128)S(1)}, u32[]{:S(2)}, u32[]{:S(2)}) async-start(f32[128,8,128]{2,1,0:T(8,128)} %get-tuple-element.13), calls=%async_computation.7 | async-start | bytes 1048576 | tf_op jit(solution)/shard_map/all_to_all | solution.py:296
  306.2 1.2 copy-start.2
  332.7 17.0 %all-to-all-start.10 = ((f32[64,8,256]{2,1,0:T(8,128)}), f32[64,8,256]{2,1,0:T(8,128)S(1)}, u32[]{:S(2)}, u32[]{:S(2)}) async-start(f32[64,8,256]{2,1,0:T(8,128)} %broadcast_in_dim.22), calls=%async_computation.10 | async-start | bytes 1048576 | tf_op jit(solution)/shard_map/all_to_all | solution.py:296
  381.7 11.6 %all-to-all-start.12 = ((f32[16,16,128]{2,1,0:T(8,128)}), f32[16,16,128]{2,1,0:T(8,128)S(1)}, u32[]{:S(2)}, u32[]{:S(2)}) async-start(f32[16,16,128]{2,1,0:T(8,128)} %bitcast.12), calls=%async_computation.12 | async-start | bytes 262144 | tf_op jit(solution)/shard_map/all_to_all | solution.py:296
Sparse Core Ops, SparseCore 0:
  30.2 99.0 all-gather.5
Sparse Core Ops, SparseCore 1:
  209.1 47.0 all-gather.3
